TPU v7x, 256 devices: a whole 4x4x8 slice. The times are simulated.
256 devices in a mesh: gx: 32 (over z, y_hi, core), gy: 8 (over y_lo, x).
Axes of the slice: x: 4, y: 4 (y_hi: 2, y_lo: 2; y = y_hi * 2 + y_lo), z: 8, core: 2. Of those that a mesh axis runs over, the one named last changes fastest.
Arguments:
- hidden_in: bfloat16 [32, 64, 20, 1024], P('gx', 'gy'), may hold values from -6 to 6
- spectral: float32 [2, 2, 20, 20, 16, 16, 128], P(None, None, None, None, 'gy', None, 'gx'), may hold values from -1.25 to 1.25
- pointwise: bfloat16 [2, 20, 20], replicated, may hold values from -1.25 to 1.25
- biases: float32 [2, 20], replicated, may hold values from -3 to 3
- upstream: bfloat16 [32, 64, 20, 1024], P('gx', 'gy'), may hold values from -6 to 6
Outputs:
- hidden_out: float32 [32, 64, 20, 1024], P('gx', 'gy')
- grad_hidden: float32 [32, 64, 20, 1024], P('gx', 'gy')
- grad_spectral: float32 [2, 2, 20, 20, 16, 16, 128], P(None, None, None, None, 'gy', None, 'gx')
- grad_pointwise: float32 [2, 20, 20], replicated
- grad_biases: float32 [2, 20], replicated
All inputs are finite; a program needn't handle non-finite values.
Results may differ from a plain program's by a relative error of at most 0.012.
The roundings to bfloat16 on the way count: a program that leaves them out, or rounds other values in their place, can miss the bound.
Values sent between devices are 32-bit elements; how exact they have to be, the bound alone decides.
No kernel may reach another device: no remote copies, remote signals or barrier semaphores. Data moves between devices by JAX's collectives and lax.ppermute only.
A program may use at most 128 MiB of HBM per device.

v0:
```python
import functools
import math

import jax
import jax.numpy as jnp
import ml_dtypes
import numpy as np
from jax import lax
from jax.experimental import pallas as pl
from jax.experimental.pallas import tpu as pltpu
from jax.sharding import Mesh, PartitionSpec as P

KX = 16
KY = 16
KZ = 16
KT = 8
NZ = 64
NT = 16
NX = 32
NY = 64
C = 20
Q = NZ * NT
ROWS = 160
PADS = (2, 3, 6, 7)

F32 = jnp.float32
BF16 = jnp.bfloat16
HIGH = lax.Precision.HIGHEST
PARAMS = pltpu.CompilerParams(vmem_limit_bytes=32 * 1024 * 1024)


def depth_tables():
    rows = np.arange(256)
    g, m4, r, mh = rows % 16, rows // 16 % 4, rows // 64 % 2, rows // 128
    m = 16 * (g // 2) + 8 * mh + 4 * (g % 2) + m4
    freq_z, freq_t = m // KT - KZ // 2, m % KT
    cells = np.arange(Q)
    phase = (freq_z[:, None] * (cells // NT) * NT + freq_t[:, None] * (cells % NT) * NZ) % Q
    angle = phase * (2.0 * np.pi / Q)
    parts = np.where(r[:, None] == 0, np.cos(angle), -np.sin(angle))
    weight = np.where(freq_t == 0, 1.0, 2.0)[:, None]
    ahead = (parts / math.sqrt(Q)).astype(np.float32).astype(ml_dtypes.bfloat16)
    behind = (parts * weight / math.sqrt(2 * KZ * KT)).astype(np.float32)
    return ahead, behind.astype(ml_dtypes.bfloat16)


def row_table(sign, factor):
    half, jj, kx = np.meshgrid(np.arange(2), np.arange(4), np.arange(KX), indexing="ij")
    x = 4 * (jj // 2) + 2 * half + jj % 2
    angle = (x * (kx - KX // 2) % NX) * (2.0 * np.pi / NX)
    pairs = np.stack([np.cos(angle), sign * np.sin(angle)], axis=-1) * factor
    pairs = pairs.astype(np.float32).astype(ml_dtypes.bfloat16).astype(np.float32)
    return pairs


def column_table():
    y = np.arange(128)[None, :] % 8
    ky = np.arange(64)[:, None] // 4
    angle = (y * (ky - KY // 2) % NY) * (2.0 * np.pi / NY)
    both = np.concatenate([np.cos(angle), np.sin(angle)], axis=0) / math.sqrt(NY)
    return both.astype(np.float32)


def iota(shape, axis):
    return lax.broadcasted_iota(jnp.int32, shape, axis)


def halves(value):
    high = value.astype(BF16)
    return high, (value - high.astype(F32)).astype(BF16)


def dot2(value, table):
    high, low = halves(value)
    return jnp.dot(high, table, preferred_element_type=F32) + jnp.dot(
        low, table, preferred_element_type=F32
    )


def dot_rows(left, right):
    return lax.dot_general(left, right, (((1,), (1,)), ((), ())), preferred_element_type=F32)


def erf(value):
    value = jnp.clip(value, -3.832506856900711, 3.832506856900711)
    square = value * value
    top = jnp.full_like(value, 0.00022905065861350646)
    for term in (0.0034082910107109506, 0.050955695062380861, 0.18520832239976145, 1.128379143519084):
        top = top * square + term
    base = jnp.full_like(value, -1.1791602954361697e-7)
    for term in (
        0.000023547966471313185,
        0.0010179625278914885,
        0.014070470171167667,
        0.11098505178285362,
        0.49746925110067538,
        1.0,
    ):
        base = base * square + term
    return value * top / base


def gelu_parts(preact):
    ramp = 0.5 * (1.0 + erf(preact * (1.0 / math.sqrt(2.0))))
    bell = jnp.exp(-0.5 * preact * preact) * (1.0 / math.sqrt(2.0 * math.pi))
    return preact * ramp, ramp + preact * bell


def compact(ref):
    return len(ref.shape) == 4


def read_main(ref, g, k):
    if compact(ref):
        return jnp.concatenate([ref[g, 2 * k], ref[g, 2 * k + 1]], axis=0)
    return ref[g, 8 * k : 8 * k + 8, :]


def read_rest(ref, g):
    if compact(ref):
        both = jnp.concatenate([ref[g, 4], ref[g, 4]], axis=0)
        return jnp.where(iota((8, 128), 0) < 4, both, pltpu.roll(both, 2, 0))
    return ref[g, 16:24, :]


def write_main(ref, g, k, value):
    if compact(ref):
        ref[g, 2 * k] = value[0:4, :]
        ref[g, 2 * k + 1] = value[4:8, :]
    else:
        ref[g, 8 * k : 8 * k + 8, :] = value


def write_rest(ref, g, value):
    if compact(ref):
        ref[g, 4] = jnp.where(iota((8, 128), 0) < 2, value, pltpu.roll(value, 6, 0))[0:4, :]
    else:
        ref[g, 16:24, :] = value


def pack(spectra, out_ref, main, rest):
    main[0:256, :] = jnp.transpose(spectra[:128, :])
    for g in range(16):
        for k in range(2):
            write_main(out_ref, g, k, main[pl.ds(128 * k + g, 8, stride=16), :])
    left, right = spectra[128:, :128], spectra[128:, 128:]
    lane = iota((32, 128), 1) % 64 // 16
    pieces = []
    for m in range(4):
        first = pltpu.roll(left, (128 - 16 * m) % 128, 1)
        second = pltpu.roll(right, (144 - 16 * m) % 128, 1)
        pieces.append(jnp.where(lane == 0, first, jnp.where(lane == 1, second, 0.0)))
    rest[0:128, :] = jnp.transpose(jnp.concatenate(pieces, axis=0))
    for g in range(16):
        write_rest(out_ref, g, rest[pl.ds(g, 8, stride=16), :])


def unpack(blocks, main, rest):
    for g in range(16):
        for k in range(2):
            main[pl.ds(128 * k + g, 8, stride=16), :] = read_main(blocks, g, k)
        rest[pl.ds(g, 8, stride=16), :] = read_rest(blocks, g)
    turned = jnp.transpose(rest[0:128, :])
    lane = iota((32, 128), 1) % 64 // 16
    left = right = jnp.zeros((32, 128), F32)
    for m in range(4):
        piece = turned[32 * m : 32 * m + 32, :]
        left = jnp.where(lane == m, pltpu.roll(piece, 16 * m, 1), left)
        right = jnp.where(lane == m, pltpu.roll(piece, (112 + 16 * m) % 128, 1), right)
    return jnp.concatenate(
        [jnp.transpose(main[0:256, :]), jnp.concatenate([left, right], axis=1)], axis=0
    )


def rotate(value, sign):
    return sign * pltpu.roll(value, 4, 0)


def turn_sign():
    return jnp.where(iota((8, 128), 0) < 4, -1.0, 1.0).astype(F32)


def pad_rows():
    return iota((8, 128), 0) % 4 >= 2


def start_kernel(field, ahead, out_ref, token, main, rest, near, table, sems):
    copies = []
    for part in range(2):
        cols = pl.ds(512 * part, 512)
        copies.append(
            (
                pltpu.make_async_copy(field.at[:, cols], near.at[part], sems.at[2 * part]),
                pltpu.make_async_copy(ahead.at[:, cols], table.at[part], sems.at[2 * part + 1]),
            )
        )
        for copy in copies[-1]:
            copy.start()
    token[...] = jnp.zeros_like(token)
    spectra = None
    for part in range(2):
        for copy in copies[part]:
            copy.wait()
        term = dot_rows(near[part], table[part])
        spectra = term if spectra is None else spectra + term
    pack(spectra, out_ref, main, rest)


def prepare_kernel(
    token, weights, table, above, far_pointwise, far_biases,
    first, second, twiddle, near_above, local_back, local_ahead, offsets,
    near, padded_rows, pointwise, biases, sems,
):
    small = [
        pltpu.make_async_copy(far_pointwise, pointwise, sems.at[2]),
        pltpu.make_async_copy(far_biases, biases, sems.at[3]),
    ]
    for copy in small:
        copy.start()
    copies = [
        pltpu.make_async_copy(weights.at[layer], near.at[layer], sems.at[layer]) for layer in range(2)
    ]
    late = [
        pltpu.make_async_copy(table, twiddle, sems.at[4]),
        pltpu.make_async_copy(above, near_above, sems.at[5]),
    ]
    for copy in copies + late:
        copy.start()
    padded_rows[...] = jnp.zeros_like(padded_rows)
    for copy in small:
        copy.wait()
    owner = (iota((ROWS, C), 0) // 8 == iota((ROWS, C), 1)).astype(F32)
    same = iota((ROWS, ROWS), 0) % 8 == iota((ROWS, ROWS), 1) % 8
    for layer in range(2):
        mixing = pointwise[layer].astype(F32)
        rows = jnp.dot(owner, mixing, precision=HIGH, preferred_element_type=F32)
        wide = lax.dot_general(
            rows, owner, (((1,), (1,)), ((), ())), precision=HIGH, preferred_element_type=F32
        )
        wide = jnp.where(same, wide, 0.0)
        local_back[layer] = wide.astype(BF16)
        padded = jnp.zeros((256, 256), F32)
        padded = jnp.concatenate(
            [
                jnp.concatenate([wide, jnp.zeros((ROWS, 96), F32)], axis=1),
                jnp.zeros((96, 256), F32),
            ],
            axis=0,
        )
        local_ahead[layer] = jnp.transpose(padded)[:ROWS, :ROWS].astype(BF16)
    offsets[...] = lax.dot_general(
        owner, biases[...], (((1,), (1,)), ((), ())), precision=HIGH, preferred_element_type=F32
    )
    for layer, out_ref in ((0, first), (1, second)):
        copies[layer].wait()
        for part in range(2):
            for c in range(C):
                slot = c % 4
                padded_rows[slot, :, 0:C] = near[layer, part, c]
                out_ref[part, c] = jnp.transpose(padded_rows[slot])[:24, :]
    for copy in late:
        copy.wait()


def entry(table, half, jj, kx):
    first, second = (jnp.where(half == 0, float(a), float(b)) for a, b in zip(*table[:, jj, kx]))
    return first, second


def x_ahead_kernel(table, blocks, *others):
    out_ref = others[-1]
    half = lax.axis_index("h")
    sign = turn_sign()
    place = iota((8, 128), 0) % 4
    for part in range(3):
        groups = [[None] * 4 for _ in range(4)]
        turned = [[None] * 4 for _ in range(4)]
        for jj in range(4):
            x0, x1, x2, x3 = (
                read_main(blocks, jj + 4 * i, part) if part < 2 else read_rest(blocks, jj + 4 * i)
                for i in range(4)
            )
            even, odd = x0 + x2, x0 - x2
            even_other, odd_other = x1 + x3, rotate(x1 - x3, sign)
            found = (even + even_other, odd - odd_other, even - even_other, odd + odd_other)
            for k in range(4):
                groups[k][jj] = found[k]
                turned[k][jj] = rotate(found[k], sign)
        modes = []
        for kx in range(KX):
            total = None
            for jj in range(4):
                real, imag = entry(table, half, jj, kx)
                term = real * groups[kx % 4][jj] + imag * turned[kx % 4][jj]
                total = term if total is None else total + term
            if part < 2:
                write_main(out_ref, part * 8 + kx // 2, kx % 2, total)
            else:
                modes.append(total)
        if part == 2:
            for k in range(8):
                first, second = modes[2 * k], modes[2 * k + 1]
                near = jnp.where(place == 0, first, pltpu.roll(second, 1, 0))
                write_rest(out_ref, k, near)
                near = jnp.where(place == 0, pltpu.roll(first, 7, 0), second)
                write_rest(out_ref, 8 + k, near)


def x_behind_kernel(table, blocks, out_ref):
    half = lax.axis_index("h")
    sign = turn_sign()
    place = iota((8, 128), 0) % 4
    sums = None if compact(blocks) else block_sums(blocks)
    for part in range(3):
        totals = [[None] * 4 for _ in range(4)]
        for kx in range(KX):
            if part < 2:
                mode = read_main(blocks, part * 8 + kx // 2, kx % 2)
            else:
                first, second = read_rest(blocks, kx // 2), read_rest(blocks, 8 + kx // 2)
                if kx % 2 == 0:
                    second = pltpu.roll(second, 1, 0)
                else:
                    first = pltpu.roll(first, 7, 0)
                mode = jnp.where(place == 0, first, jnp.where(place == 1, second, 0.0))
            turned = rotate(mode, sign)
            for jj in range(4):
                real, imag = entry(table, half, jj, kx)
                term = real * mode + imag * turned
                old = totals[kx % 4][jj]
                totals[kx % 4][jj] = term if old is None else old + term
        for jj in range(4):
            h0, h1, h2, h3 = (totals[k][jj] for k in range(4))
            even, odd = h0 + h2, h0 - h2
            even_other, odd_other = h1 + h3, rotate(h1 - h3, sign)
            found = (even + even_other, odd + odd_other, even - even_other, odd - odd_other)
            for i in range(4):
                if part < 2:
                    write_main(out_ref, jj + 4 * i, part, found[i])
                elif sums is None:
                    write_rest(out_ref, jj + 4 * i, found[i])
                else:
                    write_rest(out_ref, jj + 4 * i, jnp.where(place >= 2, sums, found[i]))


def channel_rows():
    lane = iota((32, 256), 1)
    owner = jnp.where(lane < 128, lane // 8, 16 + lane // 8 % 4)
    return (owner == iota((32, 256), 0)).astype(F32).astype(BF16)


def times(value, factor):
    return (
        value[0] * factor[0] - value[1] * factor[1],
        value[0] * factor[1] + value[1] * factor[0],
    )


def plus(one, two):
    return one[0] + two[0], one[1] + two[1]


def minus(one, two):
    return one[0] - two[0], one[1] - two[1]


def fourth(values, sign):
    even, odd = plus(values[0], values[2]), minus(values[0], values[2])
    even_other, odd_other = plus(values[1], values[3]), minus(values[1], values[3])
    turned = (-sign * odd_other[1], sign * odd_other[0])
    return plus(even, even_other), plus(odd, turned), minus(even, even_other), minus(odd, turned)


def odd_turn(y, sign):
    low = iota((8, 128), 0) < 4
    angle = math.pi * y / 4
    return jnp.where(low, 1.0, math.cos(angle)), jnp.where(low, 0.0, sign * math.sin(angle))


def y_ahead(blocks, twiddle, wide):
    low = iota((8, 128), 0) < 4
    keep = iota((8, 128), 0) % 4 == iota((8, 128), 1) // 32
    units = [[] for _ in range(4)]
    for y in range(8):
        other = read_rest(blocks, y) + read_rest(blocks, 8 + y)
        for k in range(2):
            value = read_main(blocks, y, k) + read_main(blocks, 8 + y, k)
            swapped = pltpu.roll(value, 4, 0)
            units[k].append((jnp.where(low, value, swapped), jnp.where(low, swapped, value)))
            units[2 + k].append(
                (
                    jnp.broadcast_to(other[k : k + 1, :], (8, 128)),
                    jnp.broadcast_to(other[4 + k : 5 + k, :], (8, 128)),
                )
            )
    turns = [odd_turn(y, -1.0) for y in range(8)]
    for unit in range(4):
        values = [units[unit][0]] + [times(units[unit][y], turns[y]) for y in range(1, 8)]
        groups = fourth([plus(values[n], values[n + 4]) for n in range(4)], -1.0)
        lanes = slice(0, 128) if unit < 2 else slice(128, 256)
        for pair in range(8):
            at = 8 * pair
            factor = (twiddle[at : at + 8, :], -twiddle[64 + at : 72 + at, :])
            real, imag = times(groups[pair % 4], factor)
            if unit >= 2:
                real, imag = jnp.where(keep, real, 0.0), jnp.where(keep, imag, 0.0)
            at += 64 * (unit % 2)
            wide[at : at + 8, lanes] = real
            wide[128 + at : 136 + at, lanes] = imag
    high, low_part = halves(wide[...])
    table = channel_rows()
    return dot_rows(table, high) + dot_rows(table, low_part)


def y_behind(modes, twiddle, scale, pads, wide, out_ref):
    wide[...] = dot2(jnp.transpose(modes), channel_rows())
    row = iota((8, 128), 0)
    low = row < 4
    keep = row % 4 == iota((8, 128), 1) // 32
    turns = [odd_turn(y, 1.0) for y in range(8)]
    rests = [pads] * 8
    for unit in range(4):
        k = unit % 2
        lanes = slice(0, 128) if unit < 2 else slice(128, 256)
        values = []
        for pair in range(8):
            at = 8 * pair
            factor = (twiddle[at : at + 8, :] * scale, twiddle[64 + at : 72 + at, :] * scale)
            at += 64 * k
            values.append(times((wide[at : at + 8, lanes], wide[128 + at : 136 + at, lanes]), factor))
        groups = fourth([plus(values[n], values[n + 4]) for n in range(4)], 1.0)
        for y in range(8):
            real, imag = groups[y % 4] if y == 0 else times(groups[y % 4], turns[y])
            if unit < 2:
                real = real + pltpu.roll(real, 4, 0)
                imag = imag + pltpu.roll(imag, 4, 0)
                value = jnp.where(low, real, imag)
                write_main(out_ref, y, k, value)
                write_main(out_ref, 8 + y, k, value)
            else:
                for r, value in ((0, real), (1, imag)):
                    value = jnp.where(keep, value, 0.0)
                    for step in (4, 2, 1):
                        value = value + pltpu.roll(value, step, 0)
                    rests[y] = jnp.where(row == 4 * r + k, value, rests[y])
    for y in range(8):
        write_rest(out_ref, y, rests[y])
        write_rest(out_ref, 8 + y, rests[y])


def mix_kernel(blocks, weights, twiddle, out_ref, spectrum, wide, mixed):
    spectrum[...] = y_ahead(blocks, twiddle, wide)
    out_real = out_imag = jnp.zeros((24, 128), F32)
    for c in range(C):
        first = jnp.broadcast_to(spectrum[c : c + 1, 0:128], (24, 128))
        second = jnp.broadcast_to(spectrum[c : c + 1, 128:256], (24, 128))
        w_real, w_imag = weights[0, c], weights[1, c]
        out_real += first * w_real - second * w_imag
        out_imag += first * w_imag + second * w_real
    mixed[0:24, 0:128] = out_real
    mixed[0:24, 128:256] = out_imag
    mixed[24:32, :] = jnp.zeros((8, 256), F32)
    y_behind(mixed[...], twiddle, 2.0, jnp.zeros((8, 128), F32), wide, out_ref)


def mix_grad_kernel(blocks, weights, twiddle, field, slopes, out_ref, dmixed, wide, mixed):
    sums = cell_sums(field, slopes)
    dmixed[...] = 2.0 * y_ahead(blocks, twiddle, wide)
    real, imag = dmixed[0:24, 0:128], dmixed[0:24, 128:256]
    for c in range(C):
        w_real, w_imag = weights[0, c], weights[1, c]
        mixed[c : c + 1, 0:128] = jnp.sum(w_real * real + w_imag * imag, axis=0, keepdims=True)
        mixed[c : c + 1, 128:256] = jnp.sum(w_real * imag - w_imag * real, axis=0, keepdims=True)
    mixed[C:32, :] = jnp.zeros((32 - C, 256), F32)
    y_behind(mixed[...], twiddle, 1.0, sums, wide, out_ref)


def weight_grad_body(spectrum, dmixed, out_ref, scale):
    turned, other = jnp.transpose(spectrum[...]), jnp.transpose(dmixed[...]) * scale
    for at in range(0, 128, 32):
        rows = slice(at, at + 32)
        under = slice(128 + at, 160 + at)
        real, imag = other[rows, 0:C], other[under, 0:C]
        s_real, s_imag = turned[rows, :], turned[under, :]
        for c in range(C):
            first = jnp.broadcast_to(s_real[:, c : c + 1], (32, C))
            second = jnp.broadcast_to(s_imag[:, c : c + 1], (32, C))
            out_ref[0, 0, c, rows, :] = first * real - second * imag
            out_ref[0, 1, c, rows, :] = first * imag + second * real


MODE_SCALE = math.sqrt(2.0 * KX * KY * KZ * KT / (NX * NY * NZ * NT))
CELL_SCALE = 1.0 / math.sqrt(NX * NY * NZ * NT)


def weight_grad_first(spectrum, dmixed, out_ref):
    weight_grad_body(spectrum, dmixed, out_ref, MODE_SCALE)


def weight_grad_second(spectrum, dmixed, held, out_ref):
    weight_grad_body(spectrum, dmixed, out_ref, MODE_SCALE)


def layer_kernel(blocks, field, local, offset, ahead, behind, out_ref, new_field, slope, main, rest):
    layer = 0
    high, low = halves(unpack(blocks, main, rest))
    spectra = None
    for at in range(0, Q, 256):
        cols = slice(at, at + 256)
        table = behind[:, cols]
        preact = jnp.dot(high, table, preferred_element_type=F32)
        preact += jnp.dot(low, table, preferred_element_type=F32)
        preact += jnp.dot(local[layer], field[:, cols], preferred_element_type=F32)
        preact += offset[:, layer : layer + 1]
        value, factor = gelu_parts(preact)
        value = value.astype(BF16)
        new_field[:, cols] = value
        slope[:, cols] = factor
        term = dot_rows(value, ahead[:, cols])
        spectra = term if spectra is None else spectra + term
    pack(spectra, out_ref, main, rest)


def top_kernel(blocks, field, local, offset, upstream, behind, out_ref, slopes, main, rest):
    layer = 1
    high, low = halves(unpack(blocks, main, rest))
    spectra = None
    for at in range(0, Q, 256):
        cols = slice(at, at + 256)
        table = behind[:, cols]
        preact = jnp.dot(high, table, preferred_element_type=F32)
        preact += jnp.dot(low, table, preferred_element_type=F32)
        preact += jnp.dot(local[layer], field[:, cols], preferred_element_type=F32)
        preact += offset[:, layer : layer + 1]
        factor = gelu_parts(preact)[1]
        slope = (upstream[:, cols].astype(F32) * factor).astype(BF16)
        slopes[:, cols] = slope
        term = dot_rows(slope, table)
        spectra = term if spectra is None else spectra + term
    pack(spectra, out_ref, main, rest)


def final_kernel(blocks, field, local, offset, behind, final, main, rest):
    layer = 1
    high, low = halves(unpack(blocks, main, rest))
    for at in range(0, Q, 256):
        cols = slice(at, at + 256)
        table = behind[:, cols]
        preact = jnp.dot(high, table, preferred_element_type=F32)
        preact += jnp.dot(low, table, preferred_element_type=F32)
        preact += jnp.dot(local[layer], field[:, cols], preferred_element_type=F32)
        preact += offset[:, layer : layer + 1]
        final[:, cols] = gelu_parts(preact)[0]


def block_sums(blocks):
    total = blocks[0, 16:24, :]
    for g in range(1, 16):
        total = total + blocks[g, 16:24, :]
    return jnp.where(pad_rows(), total, 0.0)


def back_kernel(
    blocks, slopes, local, factor, ahead, behind, out_ref, new_slopes, sums, main, rest
):
    layer = 1
    sums[...] = block_sums(blocks)
    high, low = halves(unpack(blocks, main, rest))
    spectra = None
    for at in range(0, Q, 256):
        cols = slice(at, at + 256)
        table = ahead[:, cols]
        grad = jnp.dot(high, table, preferred_element_type=F32)
        grad += jnp.dot(low, table, preferred_element_type=F32)
        grad += jnp.dot(local[layer], slopes[:, cols], preferred_element_type=F32)
        grad = grad.astype(BF16).astype(F32)
        slope = (grad * factor[:, cols]).astype(BF16)
        new_slopes[:, cols] = slope
        term = dot_rows(slope, behind[:, cols])
        spectra = term if spectra is None else spectra + term
    pack(spectra, out_ref, main, rest)


def end_kernel(blocks, slopes, local, ahead, later, grad_ref, mixing, offsets, main, rest):
    layer = 0
    high, low = halves(unpack(blocks, main, rest))
    for at in range(0, Q, 256):
        cols = slice(at, at + 256)
        table = ahead[:, cols]
        grad = jnp.dot(high, table, preferred_element_type=F32)
        grad += jnp.dot(low, table, preferred_element_type=F32)
        grad += jnp.dot(local[layer], slopes[:, cols], preferred_element_type=F32)
        grad_ref[:, cols] = grad
    row = iota((24, 8), 0) // 6
    col = iota((24, 8), 1)
    pick = sum(((row == i) & (col == PADS[i])).astype(F32) for i in range(4)).astype(BF16)
    place = (iota((128, 128), 0) % C == iota((128, 128), 1)).astype(F32).astype(BF16)
    keep = iota((24, 128), 1) // C == iota((24, 128), 0) % 6
    for at_layer, total in ((0, block_sums(blocks)), (1, later[...])):
        first, second = halves(total)
        wide = jnp.dot(pick, first, preferred_element_type=F32)
        wide += jnp.dot(pick, second, preferred_element_type=F32)
        found = dot2(jnp.where(keep, wide, 0.0), place) * CELL_SCALE
        for c in range(C):
            mixing[c, at_layer : at_layer + 1, :] = found[c : c + 1, 0:C]
        offsets[at_layer : at_layer + 1, :] = found[C : C + 1, 0:C]


def cell_sums(field, slopes):
    slope = slopes[...]
    pairs = jnp.concatenate(
        [dot_rows(field[...], slope), dot_rows(jnp.ones((8, Q), BF16), slope)], axis=0
    )
    pairs = jnp.where(iota((168, ROWS), 0) % 8 == iota((168, ROWS), 1) % 8, pairs, 0.0)
    lane = iota((ROWS, 128), 1)
    place = ((lane < 6 * C) & (lane % C == iota((ROWS, 128), 0) // 8)).astype(F32)
    wide = dot2(pairs, place.astype(BF16))
    wide = jnp.where(iota((168, 128), 1) // C == iota((168, 128), 0) // 8 % 6, wide, 0.0)
    row = iota((8, 168), 0)
    owner = iota((8, 168), 1) // 48
    pick = sum(((owner == i) & (row == PADS[i])).astype(F32) for i in range(4))
    pick, (high, low) = pick.astype(BF16), halves(wide)
    return jnp.dot(pick, high, preferred_element_type=F32) + jnp.dot(
        pick, low, preferred_element_type=F32
    )


VM = pl.BlockSpec(memory_space=pltpu.VMEM)
FAR = pl.BlockSpec(memory_space=pltpu.HBM)
BLOCKS = jax.ShapeDtypeStruct((16, 24, 128), F32)
SLABS = jax.ShapeDtypeStruct((16, 5, 4, 128), F32)
MODES = jax.ShapeDtypeStruct((32, 256), F32)
WIDE16 = jax.ShapeDtypeStruct((ROWS, Q), BF16)
WIDE32 = jax.ShapeDtypeStruct((ROWS, Q), F32)
SUMS = jax.ShapeDtypeStruct((8, 128), F32)
TURN = [pltpu.VMEM((272, 128), F32), pltpu.VMEM((144, 128), F32)]
MIX = [pltpu.VMEM((256, 256), F32), pltpu.VMEM((32, 256), F32)]
WEIGHTS = jax.ShapeDtypeStruct((2, C, 24, 128), F32)


def call(kernel, shapes, scratch, *operands, specs=None, cost=None, params=PARAMS):
    many = isinstance(shapes, (list, tuple))
    return pl.pallas_call(
        kernel,
        out_shape=shapes,
        in_specs=specs or [VM] * len(operands),
        out_specs=[VM] * len(shapes) if many else VM,
        scratch_shapes=scratch,
        compiler_params=params,
        cost_estimate=cost,
    )(*operands)


def far(value):
    return pltpu.with_memory_space_constraint(value, pltpu.HBM)


def swap_rows(value):
    return lax.all_to_all(value, ("z", "core"), split_axis=0, concat_axis=0, tiled=True)


def swap_cols(value):
    return lax.all_to_all(value, ("h", "ylo", "x"), split_axis=0, concat_axis=0, tiled=True)


def per_device(hidden_in, spectral, pointwise, biases, upstream):
    ahead, behind = (jnp.asarray(t) for t in depth_tables())
    root = 1.0 / math.sqrt(NX)
    to_modes = [row_table(-1.0, f) for f in (root, 0.25)]
    to_rows = [row_table(1.0, f) for f in (0.25, root)]
    field = jnp.transpose(hidden_in[0], (1, 0, 2)).reshape(ROWS, Q)
    above = jnp.transpose(upstream[0], (1, 0, 2)).reshape(ROWS, Q)
    weights = jnp.transpose(spectral, (0, 1, 2, 4, 5, 6, 3)).reshape(2, 2, C, 128, C)

    def x_step(kernel, table, shape, blocks, *after):
        return call(
            functools.partial(kernel, table), shape, [], blocks, *after,
            specs=[VM] + [FAR] * len(after),
        )

    def mix_step(kernel, shape, layer, blocks, *more):
        return call(kernel, [shape, MODES], MIX, blocks, turned[layer], twiddle, *more)

    def weight_grad(layer, spectrum, dmixed, held=None):
        out_spec = pl.BlockSpec((1, 2, C, 128, C), lambda i: (layer, 0, 0, 0, 0))
        mode_spec = pl.BlockSpec((32, 256), lambda i: (0, 0))
        operands = (spectrum, dmixed) + (() if held is None else (held,))
        return pl.pallas_call(
            weight_grad_first if held is None else weight_grad_second,
            grid=(1,),
            out_shape=jax.ShapeDtypeStruct((2, 2, C, 128, C), F32),
            in_specs=[mode_spec, mode_spec] + [pl.BlockSpec(memory_space=pl.ANY)] * (held is not None),
            out_specs=out_spec,
            input_output_aliases={} if held is None else {2: 0},
            compiler_params=PARAMS,
            cost_estimate=pl.CostEstimate(flops=2000000, bytes_accessed=3000000, transcendentals=0),
        )(*operands)

    def round_trip(blocks, step, side, *after):
        blocks = swap_rows(blocks)
        blocks = swap_cols(x_step(x_ahead_kernel, to_modes[side], SLABS, blocks, *after))
        blocks, modes = step(blocks)
        blocks = swap_cols(blocks)
        blocks = swap_rows(x_step(x_behind_kernel, to_rows[side], BLOCKS if side else SLABS, blocks))
        return blocks, modes

    loads = [
        pltpu.VMEM((2, ROWS, 512), BF16),
        pltpu.VMEM((2, 256, 512), BF16),
        pltpu.SemaphoreType.DMA((4,)),
    ]
    blocks, token = call(
        start_kernel, [SLABS, SUMS], TURN + loads, far(field), far(ahead), specs=[FAR, FAR]
    )
    squares = jax.ShapeDtypeStruct((2, ROWS, ROWS), BF16)
    first, second, twiddle, near_above, local_back, local_ahead, offsets = call(
        prepare_kernel,
        [
            WEIGHTS, WEIGHTS, jax.ShapeDtypeStruct((128, 128), F32), WIDE16,
            squares, squares, jax.ShapeDtypeStruct((ROWS, 2), F32),
        ],
        [
            pltpu.VMEM((2, 2, C, 128, C), F32),
            pltpu.VMEM((4, 128, 128), F32),
            pltpu.VMEM((2, C, C), BF16),
            pltpu.VMEM((2, C), F32),
            pltpu.SemaphoreType.DMA((6,)),
        ],
        token, *(far(a) for a in (weights, jnp.asarray(column_table()), above, pointwise, biases)),
        specs=[pl.BlockSpec(memory_space=pl.ANY)] + [FAR] * 5,
        cost=pl.CostEstimate(flops=60000000, bytes_accessed=8000000, transcendentals=0),
    )
    turned = (first, second)
    blocks, spectrum_0 = round_trip(blocks, lambda b: mix_step(mix_kernel, SLABS, 0, b), 0, twiddle)
    blocks, field_1, factor_0 = call(
        layer_kernel, [SLABS, WIDE16, WIDE32], TURN,
        blocks, field, local_ahead, offsets, ahead, behind,
    )
    blocks, spectrum_1 = round_trip(blocks, lambda b: mix_step(mix_kernel, SLABS, 1, b), 0)
    final = call(
        final_kernel, WIDE32, TURN,
        blocks, field_1, local_ahead, offsets, behind,
        cost=pl.CostEstimate(flops=200000000, bytes_accessed=2000000, transcendentals=0),
    )
    blocks, slopes_1 = call(
        top_kernel, [SLABS, WIDE16],
        TURN,
        blocks, field_1, local_ahead, offsets, near_above, behind,
    )
    blocks, dmixed_1 = round_trip(blocks, lambda b: mix_step(mix_grad_kernel, BLOCKS, 1, b, field_1, slopes_1), 1)
    grads = weight_grad(1, spectrum_1, dmixed_1)
    blocks, slopes_0, later = call(
        back_kernel, [SLABS, WIDE16, SUMS], TURN,
        blocks, slopes_1, local_back, factor_0, ahead, behind,
    )
    blocks, dmixed_0 = round_trip(blocks, lambda b: mix_step(mix_grad_kernel, BLOCKS, 0, b, field, slopes_0), 1)
    grads = weight_grad(0, spectrum_0, dmixed_0, grads)
    grad_hidden, mixing, offset_grads = call(
        end_kernel,
        [WIDE32, jax.ShapeDtypeStruct((C, 2, C), F32), jax.ShapeDtypeStruct((2, C), F32)],
        TURN,
        blocks, slopes_0, local_back, ahead, later,
    )

    def cells(value):
        return jnp.transpose(value.reshape(C, 8, Q), (1, 0, 2))[None]

    grad_spectral = jnp.transpose(grads.reshape(2, 2, C, 2, 16, 4, C), (0, 1, 2, 6, 3, 4, 5))
    return (
        cells(final),
        cells(grad_hidden),
        grad_spectral,
        jnp.transpose(mixing, (1, 0, 2)),
        offset_grads,
    )


def solution(mesh):
    names = ("z", "h", "core", "ylo", "x")
    fine = Mesh(mesh.devices.reshape(8, 2, 2, 2, 4), names)
    rows, cols = ("z", "h", "core"), ("ylo", "x")
    grid = P(rows, cols, None, None)
    modes = P(None, None, None, None, cols, None, rows)
    return jax.shard_map(
        per_device,
        mesh=fine,
        in_specs=(grid, modes, P(), P(), grid),
        out_specs=(grid, grid, modes, P(), P()),
        check_vma=False,
    )
```

profile of v0, /device:TPU:1, one launch (start us, length us, event | category | flops | bytes accessed | tf_op | source)
XLA Modules:
  0.0 217.1 jit_solution(16317369362630909717)
XLA Ops:
  0.7 2.5 %shard_map.119 = (f32[16,5,4,128]{3,2,1,0:T(4,128)}, f32[8,128]{1,0:T(8,128)S(1)}) custom-call(bf16[160,1024]{1,0:T(8,128)(2,1)} %bitcast.27, bf16[256,1024]{1,0:T(8,128)(2,1)} %constant.6.clone.ahead), custom_call_target="tpu_custom_call" | custom-call | tf_op jit(solution)/shard_map/pallas_call | solution.py:643
  3.2 10.0 %all-to-all-start = ((f32[16,5,4,128]{3,2,1,0:T(4,128)}), f32[16,5,4,128]{3,2,1,0:T(4,128)S(1)}, u32[]{:S(2)}, u32[]{:S(2)}) async-start(f32[16,5,4,128]{3,2,1,0:T(4,128)} %get-tuple-element.33), calls=%async_computation | async-start | bytes 327680 | tf_op jit(solution)/shard_map/all_to_all | solution.py:659
  14.5 3.3 %shard_map.120 = (f32[2,20,24,128]{3,2,1,0:T(8,128)S(1)}, f32[2,20,24,128]{3,2,1,0:T(8,128)S(1)}, f32[128,128]{1,0:T(8,128)S(1)}, bf16[160,1024]{1,0:T(8,128)(2,...) custom-call(f32[8,128]{1,0:T(8,128)S(1)} %get-tuple-element.34.token, ...), custom_call_target="tpu_custom_call" | custom-call | flops 60000000 | bytes 8000000 | tf_op jit(solution)/shard_map/pallas_call | solution.py:643
  18.6 4.3 %all-to-all-done.blocks = f32[16,5,4,128]{3,2,1,0:T(4,128)S(1)} async-done(((f32[16,5,4,128]{3,2,1,0:T(4,128)}), f32[16,5,4,128]{3,2,1,0:T(4,128)S(1)}, u32[]{:S(2)}, u32[]{:S(2)}) %all-to-all-start) | async-done | bytes 163872 | tf_op jit(solution)/shard_map/all_to_all | solution.py:659
  23.0 14.3 %all_to_all.80.blocks = f32[16,5,4,128]{3,2,1,0:T(4,128)S(1)} all-to-all(f32[16,5,4,128]{3,2,1,0:T(4,128)S(1)} %shard_map.121), channel_id=1, replica_groups=mesh['z'=8,'h'=2,'core'=2,'ylo'=2,'x'=4] {'h','ylo','x'}, dimensions={0} | all-to-all | bytes 327680 | tf_op jit(solution)/shard_map/all_to_all | solution.py:663
  38.2 9.6 %all_to_all.81.blocks = f32[16,5,4,128]{3,2,1,0:T(4,128)S(1)} all-to-all(f32[16,5,4,128]{3,2,1,0:T(4,128)S(1)} %get-tuple-element.37), channel_id=1, replica_groups=mesh['z'=8,'h'=2,'core'=2,'ylo'=2,'x'=4] {'h','ylo','x'}, dimensions={0} | all-to-all | bytes 327680 | tf_op jit(solution)/shard_map/all_to_all | solution.py:663
  47.9 14.7 %all_to_all.82.blocks = f32[16,5,4,128]{3,2,1,0:T(4,128)S(1)} all-to-all(f32[16,5,4,128]{3,2,1,0:T(4,128)S(1)} %shard_map.123), channel_id=1, replica_groups=mesh['z'=8,'h'=2,'core'=2,'ylo'=2,'x'=4] {'z','core'}, dimensions={0} | all-to-all | bytes 327680 | tf_op jit(solution)/shard_map/all_to_all | solution.py:659
  62.6 1.6 shard_map.124
  64.3 12.3 %all_to_all.83.blocks = f32[16,5,4,128]{3,2,1,0:T(4,128)S(1)} all-to-all(f32[16,5,4,128]{3,2,1,0:T(4,128)S(1)} %get-tuple-element.40), channel_id=1, replica_groups=mesh['z'=8,'h'=2,'core'=2,'ylo'=2,'x'=4] {'z','core'}, dimensions={0} | all-to-all | bytes 327680 | tf_op jit(solution)/shard_map/all_to_all | solution.py:659
  76.7 10.5 %all_to_all.84.blocks = f32[16,5,4,128]{3,2,1,0:T(4,128)S(1)} all-to-all(f32[16,5,4,128]{3,2,1,0:T(4,128)S(1)} %shard_map.125), channel_id=1, replica_groups=mesh['z'=8,'h'=2,'core'=2,'ylo'=2,'x'=4] {'h','ylo','x'}, dimensions={0} | all-to-all | bytes 327680 | tf_op jit(solution)/shard_map/all_to_all | solution.py:663
  88.1 9.6 %all_to_all.85.blocks = f32[16,5,4,128]{3,2,1,0:T(4,128)S(1)} all-to-all(f32[16,5,4,128]{3,2,1,0:T(4,128)S(1)} %get-tuple-element.42), channel_id=1, replica_groups=mesh['z'=8,'h'=2,'core'=2,'ylo'=2,'x'=4] {'h','ylo','x'}, dimensions={0} | all-to-all | bytes 327680 | tf_op jit(solution)/shard_map/all_to_all | solution.py:663
  97.8 14.6 %all_to_all.86.blocks = f32[16,5,4,128]{3,2,1,0:T(4,128)S(1)} all-to-all(f32[16,5,4,128]{3,2,1,0:T(4,128)S(1)} %shard_map.127), channel_id=1, replica_groups=mesh['z'=8,'h'=2,'core'=2,'ylo'=2,'x'=4] {'z','core'}, dimensions={0} | all-to-all | bytes 327680 | tf_op jit(solution)/shard_map/all_to_all | solution.py:659
  114.0 12.3 %all_to_all.87.blocks = f32[16,5,4,128]{3,2,1,0:T(4,128)S(1)} all-to-all(f32[16,5,4,128]{3,2,1,0:T(4,128)S(1)} %get-tuple-element.45), channel_id=1, replica_groups=mesh['z'=8,'h'=2,'core'=2,'ylo'=2,'x'=4] {'z','core'}, dimensions={0} | all-to-all | bytes 327680 | tf_op jit(solution)/shard_map/all_to_all | solution.py:659
  126.5 10.5 %all_to_all.88.blocks = f32[16,5,4,128]{3,2,1,0:T(4,128)S(1)} all-to-all(f32[16,5,4,128]{3,2,1,0:T(4,128)S(1)} %shard_map.130), channel_id=1, replica_groups=mesh['z'=8,'h'=2,'core'=2,'ylo'=2,'x'=4] {'h','ylo','x'}, dimensions={0} | all-to-all | bytes 327680 | tf_op jit(solution)/shard_map/all_to_all | solution.py:663
  138.3 9.8 %all_to_all.89.blocks = f32[16,24,128]{2,1,0:T(8,128)S(1)} all-to-all(f32[16,24,128]{2,1,0:T(8,128)S(1)} %get-tuple-element.47), channel_id=1, replica_groups=mesh['z'=8,'h'=2,'core'=2,'ylo'=2,'x'=4] {'h','ylo','x'}, dimensions={0} | all-to-all | bytes 393216 | tf_op jit(solution)/shard_map/all_to_all | solution.py:663
  148.3 15.2 %all_to_all.90.blocks = f32[16,24,128]{2,1,0:T(8,128)S(1)} all-to-all(f32[16,24,128]{2,1,0:T(8,128)S(1)} %shard_map.132), channel_id=1, replica_groups=mesh['z'=8,'h'=2,'core'=2,'ylo'=2,'x'=4] {'z','core'}, dimensions={0} | all-to-all | bytes 393216 | tf_op jit(solution)/shard_map/all_to_all | solution.py:659
  164.6 12.3 %all_to_all.91.blocks = f32[16,5,4,128]{3,2,1,0:T(4,128)S(1)} all-to-all(f32[16,5,4,128]{3,2,1,0:T(4,128)S(1)} %get-tuple-element.50), channel_id=1, replica_groups=mesh['z'=8,'h'=2,'core'=2,'ylo'=2,'x'=4] {'z','core'}, dimensions={0} | all-to-all | bytes 327680 | tf_op jit(solution)/shard_map/all_to_all | solution.py:659
  177.1 10.5 %all_to_all.92.blocks = f32[16,5,4,128]{3,2,1,0:T(4,128)S(1)} all-to-all(f32[16,5,4,128]{3,2,1,0:T(4,128)S(1)} %shard_map.134), channel_id=1, replica_groups=mesh['z'=8,'h'=2,'core'=2,'ylo'=2,'x'=4] {'h','ylo','x'}, dimensions={0} | all-to-all | bytes 327680 | tf_op jit(solution)/shard_map/all_to_all | solution.py:663
  188.9 10.0 %all_to_all.93.blocks = f32[16,24,128]{2,1,0:T(8,128)S(1)} all-to-all(f32[16,24,128]{2,1,0:T(8,128)S(1)} %get-tuple-element.52), channel_id=1, replica_groups=mesh['z'=8,'h'=2,'core'=2,'ylo'=2,'x'=4] {'h','ylo','x'}, dimensions={0} | all-to-all | bytes 393216 | tf_op jit(solution)/shard_map/all_to_all | solution.py:663
  199.7 5.6 %all-to-all-start.15 = ((f32[16,24,128]{2,1,0:T(8,128)}), f32[16,24,128]{2,1,0:T(8,128)S(1)}, u32[]{:S(2)}, u32[]{:S(2)}) async-start(f32[16,24,128]{2,1,0:T(8,128)} %shard_map.136), calls=%async_computation.15 | async-start | bytes 393216 | tf_op jit(solution)/shard_map/all_to_all | solution.py:659
  205.3 2.0 shard_map.128
  207.2 2.5 %shard_map.138.held = f32[2,2,20,128,20]{4,3,2,1,0:T(8,128)} custom-call(f32[32,256]{1,0:T(8,128)S(1)} %get-tuple-element.57.spectrum, f32[32,256]{1,0:T(8,128)S(1)} %get-tuple-element.58.dmixed), custom_call_target="tpu_custom_call" | custom-call | flops 2000000 | bytes 3000000 | tf_op jit(solution)/shard_map/pallas_call | solution.py:688
  209.7 2.5 %shard_map.139 = f32[2,2,20,128,20]{4,3,2,1,0:T(8,128)} custom-call(f32[32,256]{1,0:T(8,128)S(1)} %get-tuple-element.55.spectrum, f32[32,256]{1,0:T(8,128)S(1)} %get-tuple-element.56.dmixed, f32[2,2,20,128,20]{4,3,2,1,0:T(8,128)} %shard_map.138.held), custom_call_target="tpu_custom_call", output_to_operand_aliasing={{}: (2, {})} | custom-call | flops 2000000 | bytes 3000000 | tf_op jit(solution)/shard_map/pallas_call | solution.py:688
  212.1 3.5 %all-to-all-done.15.blocks = f32[16,24,128]{2,1,0:T(8,128)S(1)} async-done(((f32[16,24,128]{2,1,0:T(8,128)}), f32[16,24,128]{2,1,0:T(8,128)S(1)}, u32[]{:S(2)}, u32[]{:S(2)}) %all-to-all-start.15) | async-done | bytes 196640 | tf_op jit(solution)/shard_map/all_to_all | solution.py:659
  (26 shorter events, 12.4 us)
Async XLA Ops:
  0.6 62.0 %copy-start = (bf16[256,1024]{1,0:T(8,128)(2,1)S(1)}, bf16[256,1024]{1,0:T(8,128)(2,1)}, u32[]{:S(2)}) copy-start(bf16[256,1024]{1,0:T(8,128)(2,1)} %constant.6.clone.ahead) | copy-start | bytes 1572868
  0.6 62.0 %copy-start.1 = (bf16[256,1024]{1,0:T(8,128)(2,1)S(1)}, bf16[256,1024]{1,0:T(8,128)(2,1)}, u32[]{:S(2)}) copy-start(bf16[256,1024]{1,0:T(8,128)(2,1)} %constant.7.clone.behind) | copy-start | bytes 1572868
  0.7 62.0 %copy-start.2 = (bf16[1,8,20,1024]{3,1,2,0:T(8,128)(2,1)S(1)}, bf16[1,8,20,1024]{3,1,2,0:T(8,128)(2,1)}, u32[]{:S(2)}) copy-start(bf16[1,8,20,1024]{3,1,2,0:T(8,128)(2,1)} %param.8) | copy-start | bytes 983044
  3.2 19.6 %all-to-all-start = ((f32[16,5,4,128]{3,2,1,0:T(4,128)}), f32[16,5,4,128]{3,2,1,0:T(4,128)S(1)}, u32[]{:S(2)}, u32[]{:S(2)}) async-start(f32[16,5,4,128]{3,2,1,0:T(4,128)} %get-tuple-element.33), calls=%async_computation | async-start | bytes 327680 | tf_op jit(solution)/shard_map/all_to_all | solution.py:659
  17.9 0.7 copy-start.3
  22.9 89.5 %copy-start.4 = (bf16[160,1024]{1,0:T(8,128)(2,1)S(1)}, bf16[160,1024]{1,0:T(8,128)(2,1)}, u32[]{:S(2)}) copy-start(bf16[160,1024]{1,0:T(8,128)(2,1)} %copy-done.3) | copy-start | bytes 983044
  199.7 15.9 %all-to-all-start.15 = ((f32[16,24,128]{2,1,0:T(8,128)}), f32[16,24,128]{2,1,0:T(8,128)S(1)}, u32[]{:S(2)}, u32[]{:S(2)}) async-start(f32[16,24,128]{2,1,0:T(8,128)} %shard_map.136), calls=%async_computation.15 | async-start | bytes 393216 | tf_op jit(solution)/shard_map/all_to_all | solution.py:659
where the time goes:
time: 218 us; the launch traced here: 217 us
  blocking collectives  166 us (76%)
  Pallas kernels  24.7 us (11%)
  starting transfers between devices  15.6 us (7%)
  waiting for transfers between devices  7.76 us (4%)
    all_to_all x8, blocking collectives, swap_cols(): lax.all_to_all(value, ('h', 'ylo', 'x'), split_axis=0, concat_axis=0, til...  84.8 us
    all_to_all x6, blocking collectives, swap_rows(): lax.all_to_all(value, ('z', 'core'), split_axis=0, concat_axis=0, tiled=T...  81.4 us
    pallas_call x19, Pallas kernels, call(): pl.pallas_call(kernel, out_shape=shapes, in_specs=specs or [VM] * len(ope...  19.8 us
    all_to_all x2, starting transfers between devices, swap_rows(): lax.all_to_all(value, ('z', 'core'), split_axis=0, concat_axis=0, tiled=T...  15.6 us
    all_to_all x2, waiting for transfers between devices, swap_rows(): lax.all_to_all(value, ('z', 'core'), split_axis=0, concat_axis=0, tiled=T...  7.76 us
    pallas_call x2, Pallas kernels, weight_grad(): pl.pallas_call(weight_grad_first if held is None else weight_grad_second,...  4.93 us
  transfers between devices with their start and end apart: 2, of which 2 were waited for; matrix products, arithmetic and copies ran while one was open for 1% of the time, Pallas kernels for 5%

commit v1 on v0

--- a/solution.py
+++ b/solution.py
@@ -476,17 +476,25 @@
 
 
 def weight_grad_body(spectrum, dmixed, out_ref, scale):
+    for group in range(4):
+        pl.when(pl.program_id(0) == group)(
+            functools.partial(weight_grad_group, group, spectrum, dmixed, out_ref, scale)
+        )
+
+
+def weight_grad_group(group, spectrum, dmixed, out_ref, scale):
     turned, other = jnp.transpose(spectrum[...]), jnp.transpose(dmixed[...]) * scale
     for at in range(0, 128, 32):
         rows = slice(at, at + 32)
         under = slice(128 + at, 160 + at)
         real, imag = other[rows, 0:C], other[under, 0:C]
         s_real, s_imag = turned[rows, :], turned[under, :]
-        for c in range(C):
+        for place in range(5):
+            c = 5 * group + place
             first = jnp.broadcast_to(s_real[:, c : c + 1], (32, C))
             second = jnp.broadcast_to(s_imag[:, c : c + 1], (32, C))
-            out_ref[0, 0, c, rows, :] = first * real - second * imag
-            out_ref[0, 1, c, rows, :] = first * imag + second * real
+            out_ref[0, 0, place, rows, :] = first * real - second * imag
+            out_ref[0, 1, place, rows, :] = first * imag + second * real
 
 
 MODE_SCALE = math.sqrt(2.0 * KX * KY * KZ * KT / (NX * NY * NZ * NT))
@@ -682,12 +690,12 @@
         return call(kernel, [shape, MODES], MIX, blocks, turned[layer], twiddle, *more)
 
     def weight_grad(layer, spectrum, dmixed, held=None):
-        out_spec = pl.BlockSpec((1, 2, C, 128, C), lambda i: (layer, 0, 0, 0, 0))
+        out_spec = pl.BlockSpec((1, 2, 5, 128, C), lambda i: (layer, 0, i, 0, 0))
         mode_spec = pl.BlockSpec((32, 256), lambda i: (0, 0))
         operands = (spectrum, dmixed) + (() if held is None else (held,))
         return pl.pallas_call(
             weight_grad_first if held is None else weight_grad_second,
-            grid=(1,),
+            grid=(4,),
             out_shape=jax.ShapeDtypeStruct((2, 2, C, 128, C), F32),
             in_specs=[mode_spec, mode_spec] + [pl.BlockSpec(memory_space=pl.ANY)] * (held is not None),
             out_specs=out_spec,

time: 218 us -> 218 us (level)
  no operation moved by 1% of the time
where the time goes in v1:
time: 218 us; the launch traced here: 217 us
  blocking collectives  166 us (76%)
  Pallas kernels  25.5 us (12%)
  starting transfers between devices  15.6 us (7%)
  waiting for transfers between devices  7.04 us (3%)
    all_to_all x8, blocking collectives, swap_cols(): lax.all_to_all(value, ('h', 'ylo', 'x'), split_axis=0, concat_axis=0, til...  84.8 us
    all_to_all x6, blocking collectives, swap_rows(): lax.all_to_all(value, ('z', 'core'), split_axis=0, concat_axis=0, tiled=T...  81.4 us
    pallas_call x19, Pallas kernels, call(): pl.pallas_call(kernel, out_shape=shapes, in_specs=specs or [VM] * len(ope...  19.8 us
    all_to_all x2, starting transfers between devices, swap_rows(): lax.all_to_all(value, ('z', 'core'), split_axis=0, concat_axis=0, tiled=T...  15.6 us
    all_to_all x2, waiting for transfers between devices, swap_rows(): lax.all_to_all(value, ('z', 'core'), split_axis=0, concat_axis=0, tiled=T...  7.04 us
    pallas_call x2, Pallas kernels, weight_grad(): pl.pallas_call(weight_grad_first if held is None else weight_grad_second,...  5.64 us
  transfers between devices with their start and end apart: 2, of which 2 were waited for; matrix products, arithmetic and copies ran while one was open for 1% of the time, Pallas kernels for 5%

profile of v1, /device:TPU:1, one launch (start us, length us, event | category | flops | bytes accessed | tf_op | source)
XLA Modules:
  0.0 217.1 jit_solution(16453641411266823209)
XLA Ops:
  0.7 2.5 %shard_map.119 = (f32[16,5,4,128]{3,2,1,0:T(4,128)}, f32[8,128]{1,0:T(8,128)S(1)}) custom-call(bf16[160,1024]{1,0:T(8,128)(2,1)} %bitcast.27, bf16[256,1024]{1,0:T(8,128)(2,1)} %constant.6.clone.ahead), custom_call_target="tpu_custom_call" | custom-call | tf_op jit(solution)/shard_map/pallas_call | solution.py:651
  3.2 10.0 %all-to-all-start = ((f32[16,5,4,128]{3,2,1,0:T(4,128)}), f32[16,5,4,128]{3,2,1,0:T(4,128)S(1)}, u32[]{:S(2)}, u32[]{:S(2)}) async-start(f32[16,5,4,128]{3,2,1,0:T(4,128)} %get-tuple-element.33), calls=%async_computation | async-start | bytes 327680 | tf_op jit(solution)/shard_map/all_to_all | solution.py:667
  14.5 3.3 %shard_map.120 = (f32[2,20,24,128]{3,2,1,0:T(8,128)S(1)}, f32[2,20,24,128]{3,2,1,0:T(8,128)S(1)}, f32[128,128]{1,0:T(8,128)S(1)}, bf16[160,1024]{1,0:T(8,128)(2,...) custom-call(f32[8,128]{1,0:T(8,128)S(1)} %get-tuple-element.34.token, ...), custom_call_target="tpu_custom_call" | custom-call | flops 60000000 | bytes 8000000 | tf_op jit(solution)/shard_map/pallas_call | solution.py:651
  18.6 4.3 %all-to-all-done.blocks = f32[16,5,4,128]{3,2,1,0:T(4,128)S(1)} async-done(((f32[16,5,4,128]{3,2,1,0:T(4,128)}), f32[16,5,4,128]{3,2,1,0:T(4,128)S(1)}, u32[]{:S(2)}, u32[]{:S(2)}) %all-to-all-start) | async-done | bytes 163872 | tf_op jit(solution)/shard_map/all_to_all | solution.py:667
  23.0 14.3 %all_to_all.80.blocks = f32[16,5,4,128]{3,2,1,0:T(4,128)S(1)} all-to-all(f32[16,5,4,128]{3,2,1,0:T(4,128)S(1)} %shard_map.121), channel_id=1, replica_groups=mesh['z'=8,'h'=2,'core'=2,'ylo'=2,'x'=4] {'h','ylo','x'}, dimensions={0} | all-to-all | bytes 327680 | tf_op jit(solution)/shard_map/all_to_all | solution.py:671
  38.2 9.6 %all_to_all.81.blocks = f32[16,5,4,128]{3,2,1,0:T(4,128)S(1)} all-to-all(f32[16,5,4,128]{3,2,1,0:T(4,128)S(1)} %get-tuple-element.37), channel_id=1, replica_groups=mesh['z'=8,'h'=2,'core'=2,'ylo'=2,'x'=4] {'h','ylo','x'}, dimensions={0} | all-to-all | bytes 327680 | tf_op jit(solution)/shard_map/all_to_all | solution.py:671
  47.9 14.7 %all_to_all.82.blocks = f32[16,5,4,128]{3,2,1,0:T(4,128)S(1)} all-to-all(f32[16,5,4,128]{3,2,1,0:T(4,128)S(1)} %shard_map.123), channel_id=1, replica_groups=mesh['z'=8,'h'=2,'core'=2,'ylo'=2,'x'=4] {'z','core'}, dimensions={0} | all-to-all | bytes 327680 | tf_op jit(solution)/shard_map/all_to_all | solution.py:667
  62.6 1.6 shard_map.124
  64.3 12.3 %all_to_all.83.blocks = f32[16,5,4,128]{3,2,1,0:T(4,128)S(1)} all-to-all(f32[16,5,4,128]{3,2,1,0:T(4,128)S(1)} %get-tuple-element.40), channel_id=1, replica_groups=mesh['z'=8,'h'=2,'core'=2,'ylo'=2,'x'=4] {'z','core'}, dimensions={0} | all-to-all | bytes 327680 | tf_op jit(solution)/shard_map/all_to_all | solution.py:667
  76.7 10.5 %all_to_all.84.blocks = f32[16,5,4,128]{3,2,1,0:T(4,128)S(1)} all-to-all(f32[16,5,4,128]{3,2,1,0:T(4,128)S(1)} %shard_map.125), channel_id=1, replica_groups=mesh['z'=8,'h'=2,'core'=2,'ylo'=2,'x'=4] {'h','ylo','x'}, dimensions={0} | all-to-all | bytes 327680 | tf_op jit(solution)/shard_map/all_to_all | solution.py:671
  88.1 9.6 %all_to_all.85.blocks = f32[16,5,4,128]{3,2,1,0:T(4,128)S(1)} all-to-all(f32[16,5,4,128]{3,2,1,0:T(4,128)S(1)} %get-tuple-element.42), channel_id=1, replica_groups=mesh['z'=8,'h'=2,'core'=2,'ylo'=2,'x'=4] {'h','ylo','x'}, dimensions={0} | all-to-all | bytes 327680 | tf_op jit(solution)/shard_map/all_to_all | solution.py:671
  97.8 14.6 %all_to_all.86.blocks = f32[16,5,4,128]{3,2,1,0:T(4,128)S(1)} all-to-all(f32[16,5,4,128]{3,2,1,0:T(4,128)S(1)} %shard_map.127), channel_id=1, replica_groups=mesh['z'=8,'h'=2,'core'=2,'ylo'=2,'x'=4] {'z','core'}, dimensions={0} | all-to-all | bytes 327680 | tf_op jit(solution)/shard_map/all_to_all | solution.py:667
  114.0 12.3 %all_to_all.87.blocks = f32[16,5,4,128]{3,2,1,0:T(4,128)S(1)} all-to-all(f32[16,5,4,128]{3,2,1,0:T(4,128)S(1)} %get-tuple-element.45), channel_id=1, replica_groups=mesh['z'=8,'h'=2,'core'=2,'ylo'=2,'x'=4] {'z','core'}, dimensions={0} | all-to-all | bytes 327680 | tf_op jit(solution)/shard_map/all_to_all | solution.py:667
  126.5 10.5 %all_to_all.88.blocks = f32[16,5,4,128]{3,2,1,0:T(4,128)S(1)} all-to-all(f32[16,5,4,128]{3,2,1,0:T(4,128)S(1)} %shard_map.130), channel_id=1, replica_groups=mesh['z'=8,'h'=2,'core'=2,'ylo'=2,'x'=4] {'h','ylo','x'}, dimensions={0} | all-to-all | bytes 327680 | tf_op jit(solution)/shard_map/all_to_all | solution.py:671
  138.3 9.8 %all_to_all.89.blocks = f32[16,24,128]{2,1,0:T(8,128)S(1)} all-to-all(f32[16,24,128]{2,1,0:T(8,128)S(1)} %get-tuple-element.47), channel_id=1, replica_groups=mesh['z'=8,'h'=2,'core'=2,'ylo'=2,'x'=4] {'h','ylo','x'}, dimensions={0} | all-to-all | bytes 393216 | tf_op jit(solution)/shard_map/all_to_all | solution.py:671
  148.3 15.2 %all_to_all.90.blocks = f32[16,24,128]{2,1,0:T(8,128)S(1)} all-to-all(f32[16,24,128]{2,1,0:T(8,128)S(1)} %shard_map.132), channel_id=1, replica_groups=mesh['z'=8,'h'=2,'core'=2,'ylo'=2,'x'=4] {'z','core'}, dimensions={0} | all-to-all | bytes 393216 | tf_op jit(solution)/shard_map/all_to_all | solution.py:667
  164.6 12.3 %all_to_all.91.blocks = f32[16,5,4,128]{3,2,1,0:T(4,128)S(1)} all-to-all(f32[16,5,4,128]{3,2,1,0:T(4,128)S(1)} %get-tuple-element.50), channel_id=1, replica_groups=mesh['z'=8,'h'=2,'core'=2,'ylo'=2,'x'=4] {'z','core'}, dimensions={0} | all-to-all | bytes 327680 | tf_op jit(solution)/shard_map/all_to_all | solution.py:667
  177.1 10.5 %all_to_all.92.blocks = f32[16,5,4,128]{3,2,1,0:T(4,128)S(1)} all-to-all(f32[16,5,4,128]{3,2,1,0:T(4,128)S(1)} %shard_map.134), channel_id=1, replica_groups=mesh['z'=8,'h'=2,'core'=2,'ylo'=2,'x'=4] {'h','ylo','x'}, dimensions={0} | all-to-all | bytes 327680 | tf_op jit(solution)/shard_map/all_to_all | solution.py:671
  188.9 10.0 %all_to_all.93.blocks = f32[16,24,128]{2,1,0:T(8,128)S(1)} all-to-all(f32[16,24,128]{2,1,0:T(8,128)S(1)} %get-tuple-element.52), channel_id=1, replica_groups=mesh['z'=8,'h'=2,'core'=2,'ylo'=2,'x'=4] {'h','ylo','x'}, dimensions={0} | all-to-all | bytes 393216 | tf_op jit(solution)/shard_map/all_to_all | solution.py:671
  199.7 5.6 %all-to-all-start.15 = ((f32[16,24,128]{2,1,0:T(8,128)}), f32[16,24,128]{2,1,0:T(8,128)S(1)}, u32[]{:S(2)}, u32[]{:S(2)}) async-start(f32[16,24,128]{2,1,0:T(8,128)} %shard_map.136), calls=%async_computation.15 | async-start | bytes 393216 | tf_op jit(solution)/shard_map/all_to_all | solution.py:667
  205.3 2.0 shard_map.128
  207.2 2.8 %shard_map.138.held = f32[2,2,20,128,20]{4,3,2,1,0:T(8,128)} custom-call(f32[32,256]{1,0:T(8,128)S(1)} %get-tuple-element.57.spectrum, f32[32,256]{1,0:T(8,128)S(1)} %get-tuple-element.58.dmixed), custom_call_target="tpu_custom_call" | custom-call | flops 2000000 | bytes 3000000 | tf_op jit(solution)/shard_map/pallas_call | solution.py:696
  210.0 2.8 %shard_map.139 = f32[2,2,20,128,20]{4,3,2,1,0:T(8,128)} custom-call(f32[32,256]{1,0:T(8,128)S(1)} %get-tuple-element.55.spectrum, f32[32,256]{1,0:T(8,128)S(1)} %get-tuple-element.56.dmixed, f32[2,2,20,128,20]{4,3,2,1,0:T(8,128)} %shard_map.138.held), custom_call_target="tpu_custom_call", output_to_operand_aliasing={{}: (2, {})} | custom-call | flops 2000000 | bytes 3000000 | tf_op jit(solution)/shard_map/pallas_call | solution.py:696
  212.8 2.8 %all-to-all-done.15.blocks = f32[16,24,128]{2,1,0:T(8,128)S(1)} async-done(((f32[16,24,128]{2,1,0:T(8,128)}), f32[16,24,128]{2,1,0:T(8,128)S(1)}, u32[]{:S(2)}, u32[]{:S(2)}) %all-to-all-start.15) | async-done | bytes 196640 | tf_op jit(solution)/shard_map/all_to_all | solution.py:667
  (26 shorter events, 12.4 us)
Async XLA Ops:
  0.6 62.0 %copy-start = (bf16[256,1024]{1,0:T(8,128)(2,1)S(1)}, bf16[256,1024]{1,0:T(8,128)(2,1)}, u32[]{:S(2)}) copy-start(bf16[256,1024]{1,0:T(8,128)(2,1)} %constant.6.clone.ahead) | copy-start | bytes 1572868
  0.6 62.0 %copy-start.1 = (bf16[256,1024]{1,0:T(8,128)(2,1)S(1)}, bf16[256,1024]{1,0:T(8,128)(2,1)}, u32[]{:S(2)}) copy-start(bf16[256,1024]{1,0:T(8,128)(2,1)} %constant.7.clone.behind) | copy-start | bytes 1572868
  0.7 62.0 %copy-start.2 = (bf16[1,8,20,1024]{3,1,2,0:T(8,128)(2,1)S(1)}, bf16[1,8,20,1024]{3,1,2,0:T(8,128)(2,1)}, u32[]{:S(2)}) copy-start(bf16[1,8,20,1024]{3,1,2,0:T(8,128)(2,1)} %param.8) | copy-start | bytes 983044
  3.2 19.6 %all-to-all-start = ((f32[16,5,4,128]{3,2,1,0:T(4,128)}), f32[16,5,4,128]{3,2,1,0:T(4,128)S(1)}, u32[]{:S(2)}, u32[]{:S(2)}) async-start(f32[16,5,4,128]{3,2,1,0:T(4,128)} %get-tuple-element.33), calls=%async_computation | async-start | bytes 327680 | tf_op jit(solution)/shard_map/all_to_all | solution.py:667
  17.9 0.7 copy-start.3
  22.9 89.5 %copy-start.4 = (bf16[160,1024]{1,0:T(8,128)(2,1)S(1)}, bf16[160,1024]{1,0:T(8,128)(2,1)}, u32[]{:S(2)}) copy-start(bf16[160,1024]{1,0:T(8,128)(2,1)} %copy-done.3) | copy-start | bytes 983044
  199.7 15.9 %all-to-all-start.15 = ((f32[16,24,128]{2,1,0:T(8,128)}), f32[16,24,128]{2,1,0:T(8,128)S(1)}, u32[]{:S(2)}, u32[]{:S(2)}) async-start(f32[16,24,128]{2,1,0:T(8,128)} %shard_map.136), calls=%async_computation.15 | async-start | bytes 393216 | tf_op jit(solution)/shard_map/all_to_all | solution.py:667
